TPU v7x, 256 devices: a whole 4x4x8 slice. The times are simulated.
256 devices in a mesh: seq: 32 (over y, z), head: 8 (over x, core).
Axes of the slice: x: 4, y: 4, z: 8, core: 2. Of those that a mesh axis runs over, the one named last changes fastest.
Arguments:
- vertex_features: bfloat16 [262144, 512], P(('seq', 'head')), may hold values from -48 to 48
- entry_rescaling_gain: float32 [512], replicated, may hold values from 0.1 to 1.9
- sharpness_factor: float32 [8], replicated, may hold values from 4 to 20
- triple_projection_matrix: bfloat16 [512, 3, 512], P(None, None, 'head'), may hold values from -0.25 to 0.25
- final_projection_matrix: bfloat16 [512, 512], replicated, may hold values from -0.25 to 0.25
- occupied_tile_targets: int32 [2048, 12], P('seq'), may hold values from 0 to 2047, as said below
Outputs:
- mixed: bfloat16 [262144, 512], P(('seq', 'head'))
Inputs may be any that keep to these rules, and one draw needn't show every extreme that they name: `occupied_tile_targets`: each block row lists 12 different column blocks, among them its own block, and exactly 10 of them lie in its own group (block rows g * 64 to g * 64 + 63 form group g). The block rows of one group together list at most 6 entries that lie in any one other group.
All inputs are finite; a program needn't handle non-finite values.
Results may differ from a plain program's by a relative error of at most 0.0091.
Values may be sent and summed in bfloat16 or wider, within the bound.
A program may use at most 64 MiB of HBM per device.

v0:
```python
import math
import jax
import jax.numpy as jnp
from jax import lax
from jax.experimental import pallas as pl
from jax.experimental.pallas import tpu as pltpu
from jax.sharding import PartitionSpec as P

MESH = pl.DeviceIdType.MESH
BF = jnp.bfloat16
F32 = jnp.float32
GROUPS = 32
PARTS = 8
PAIRS = 4
WIDTH = 64
BLK = 128
KB = 12
KL = 10
FAR = 2
CAP = 6
HALF = 3
RING = 8
ROWS = 8
GROUP_BLOCKS = 64
SUB = 16
CHUNKS = 4
LANES = 128
TOGETHER = 4
FINISH = 4
LOG2E = math.log2(math.e)
EPS = 1e-06


def wait_bytes(ref, sem):
    pltpu.make_async_copy(ref, ref, sem).wait()


def kernel(
    x_ref, gain_ref, w_ref, targets_ref, sharp_ref,
    out_ref,
    x_all, w_all, wk, wv, wq, kp, vp, kf, vf, q_all, num, den,
    xa0, xa1, xa2, xa3, zr0, zr1, zr2, zr3a, zr3b,
    x_in,
    zs, xs, xs3, xr, xr3, listing, req, rq, rqs, tab, tabs,
    xa_ss, xa_rs, rq_ss, rq_rs, rq_ls, tab_ls, w_ss, w_rs, ag_ss, ag_rs, z_ss, z_rs, xr_ss, xr_rs, far_rs, in_ls,
):
    me = lax.axis_index("seq")
    mh = lax.axis_index("head")
    core = lax.rem(mh, 2)
    right = lax.rem(mh + 2, PARTS)
    left = lax.rem(mh + 6, PARTS)
    opp = lax.rem(mh + 4, PARTS)
    sib = mh + 1 - 2 * core
    sib_right = right + 1 - 2 * core
    sib_left = left + 1 - 2 * core
    sib_opp = opp + 1 - 2 * core
    xas = (xa0, xa1, xa2, xa3)
    zrs = (zr0, zr1, zr2, zr3a, zr3b)

    barrier = pltpu.get_barrier_semaphore()
    load_x = pltpu.make_async_copy(x_ref, x_in, in_ls.at[0])
    load_w = pltpu.make_async_copy(w_ref, w_all.at[mh], in_ls.at[1])
    load_x.start()
    load_w.start()

    def greet_seq(d, carry):
        pl.semaphore_signal(barrier, inc=1, device_id={"seq": lax.rem(me + d, GROUPS)}, device_id_type=MESH)
        return carry

    def greet_head(d, carry):
        pl.semaphore_signal(barrier, inc=1, device_id={"head": lax.rem(mh + d, PARTS)}, device_id_type=MESH)
        return carry

    lax.fori_loop(1, GROUPS, greet_seq, 0)
    lax.fori_loop(1, PARTS, greet_head, 0)

    gain = gain_ref[...]

    def norm_block(i, carry):
        rows = x_in[pl.ds(pl.multiple_of(i * BLK, BLK), BLK), :].astype(F32)
        scale = lax.rsqrt(jnp.mean(rows * rows, axis=-1, keepdims=True) + EPS)
        x_all[mh, i] = (rows * scale * gain).astype(BF)
        return carry

    load_x.wait()
    lax.fori_loop(0, ROWS, norm_block, 0)

    pl.semaphore_wait(barrier, GROUPS - 1 + PARTS - 1)

    def send_sub(c):
        def go(d, carry):
            t = lax.rem(mh + d, PARTS)
            pltpu.make_async_remote_copy(
                src_ref=x_all.at[mh, :, pl.ds(pl.multiple_of(t * SUB, SUB), SUB), pl.ds(c * LANES, LANES)],
                dst_ref=xas[c].at[pl.ds(mh * ROWS, ROWS)],
                send_sem=xa_ss.at[c], recv_sem=xa_rs.at[c],
                device_id={"head": t}, device_id_type=MESH,
            ).start()
            return carry

        lax.fori_loop(1, PARTS, go, 0)
        xas[c][pl.ds(mh * ROWS, ROWS)] = x_all[
            mh, :, pl.ds(pl.multiple_of(mh * SUB, SUB), SUB), pl.ds(c * LANES, LANES)]

    send_sub(0)

    listing[...] = jnp.full(listing.shape, -GROUP_BLOCKS, jnp.int32)
    listing[0:KB, 0:GROUP_BLOCKS] = targets_ref[...]
    lane = lax.broadcasted_iota(jnp.int32, (1, LANES), 1)
    none = jnp.zeros((1, LANES), jnp.int32)
    near_count, far_count = none, none
    near_rows = [none] * KL
    owners, withins = [none] * FAR, [none] * FAR
    for j in range(KB):
        target = listing[j:j + 1, :]
        owner = lax.shift_right_arithmetic(target, 6)
        within = target - owner * GROUP_BLOCKS
        is_far = owner != me
        for k in range(KL):
            near_rows[k] = jnp.where(jnp.logical_and(owner == me, near_count == k), within, near_rows[k])
        for k in range(FAR):
            here = jnp.logical_and(is_far, far_count == k)
            owners[k] = jnp.where(here, owner, owners[k])
            withins[k] = jnp.where(here, within, withins[k])
        near_count = near_count + jnp.where(is_far, 0, 1)
        far_count = far_count + jnp.where(is_far, 1, 0)
    group = lax.broadcasted_iota(jnp.int32, (GROUPS, LANES), 0)
    hits = [jnp.where(group == owners[k], 1, 0) for k in range(FAR)]
    both = hits[0] + hits[1]
    counted = both
    wide_lane = lax.broadcasted_iota(jnp.int32, (GROUPS, LANES), 1)
    for step in (1, 2, 4, 8, 16, 32):
        counted = counted + jnp.where(wide_lane >= step, pltpu.roll(counted, step, 1), 0)
    counted = counted - both

    def over_groups(value):
        eight = value[0:8] + value[8:16] + value[16:24] + value[24:32]
        four = eight[0:4] + eight[4:8]
        two = four[0:2] + four[2:4]
        return two[0:1] + two[1:2]

    slots = [over_groups(hits[0] * counted), over_groups(hits[1] * (counted + hits[0]))]
    wanted = jnp.zeros((GROUPS, LANES), jnp.int32)
    for c in range(CAP):
        one = none
        for k in range(FAR):
            one = one + hits[k] * jnp.where(slots[k] == c, withins[k], 0)
        for step in (1, 2, 4, 8, 16, 32, 64):
            one = one + pltpu.roll(one, step, 1)
        wanted = jnp.where(wide_lane == c, one, wanted)
    for o in range(GROUPS):
        req[o] = wanted[o:o + 1, :]
    rq[me] = req[me]

    def send_req(d, carry):
        t = lax.rem(me + d, GROUPS)
        pltpu.make_async_remote_copy(
            src_ref=req.at[t], dst_ref=rq.at[me], send_sem=rq_ss, recv_sem=rq_rs,
            device_id={"seq": t}, device_id_type=MESH,
        ).start()
        return carry

    lax.fori_loop(1, GROUPS, send_req, 0)

    for k in range(KL):
        tab[k:k + 1, :] = near_rows[k]
    for k in range(FAR):
        tab[KL + k:KL + k + 1, :] = owners[k] * CAP + slots[k]
    tab[KB:16, :] = jnp.zeros((16 - KB, LANES), jnp.int32)
    to_tabs = pltpu.make_async_copy(tab, tabs, tab_ls)
    to_tabs.start()

    low = lane < WIDTH
    load_w.wait()

    def ring(buf, ss, rs, half):
        first, second = pl.ds(0, half), pl.ds(half, half)

        def copy(k, view, to):
            return pltpu.make_async_remote_copy(
                src_ref=view, dst_ref=view, send_sem=ss.at[k], recv_sem=rs.at[k],
                device_id={"head": to}, device_id_type=MESH)

        return (
            copy(0, buf.at[mh], right), copy(1, buf.at[mh], left), copy(2, buf.at[mh], sib),
            copy(3, buf.at[left, first], right), copy(4, buf.at[right, second], left),
            copy(5, buf.at[left], sib), copy(6, buf.at[right], sib), copy(7, buf.at[opp], sib),
        )

    w_ring = ring(w_all, w_ss, w_rs, w_all.shape[1] // 2)
    x_ring = ring(x_all, ag_ss, ag_rs, ROWS // 2)

    for k in (0, 1, 2):
        w_ring[k].start()
    for c in range(1, CHUNKS):
        send_sub(c)
    for k in (0, 1, 2):
        x_ring[k].start()

    wait_bytes(rq.at[pl.ds(0, GROUPS - 1)], rq_rs)
    to_smem = pltpu.make_async_copy(rq, rqs, rq_ls)
    to_smem.start()
    to_smem.wait()

    def send_slots(c, k, t, first, count):
        pltpu.make_async_remote_copy(
            src_ref=zs.at[c, pl.ds(first + t * count, count)], dst_ref=zrs[k].at[pl.ds(me * count, count)],
            send_sem=z_ss.at[k], recv_sem=z_rs.at[k],
            device_id={"seq": t}, device_id_type=MESH,
        ).start()

    def send_groups(c):
        wait_bytes(xas[c].at[pl.ds(0, GROUP_BLOCKS - ROWS)], xa_rs.at[c])

        def one(dy, dz):
            t = lax.rem(me // RING + dy, GROUPS // RING) * RING + lax.rem(me + dz, RING)
            if c < CHUNKS - 1:
                for s in range(CAP):
                    zs[c, t * CAP + s] = xas[c][rqs[t, 0, s]]
                send_slots(c, c, t, 0, CAP)
                return
            for s in range(HALF):
                a = xas[c][rqs[t, 0, 2 * s]].astype(F32)
                b = xas[c][rqs[t, 0, 2 * s + 1]].astype(F32)
                zs[c, t * HALF + s] = jnp.concatenate([a[0:8], b[0:8]], axis=0).astype(BF)
                zs[c, GROUPS * HALF + t * HALF + s] = jnp.concatenate([a[8:16], b[8:16]], axis=0).astype(BF)
            send_slots(c, c, t, 0, HALF)

        def go(i, carry):
            dz = jnp.where(i % 2 == 0, 1 + i // 2, RING - 1 - i // 2)
            for dy in (0, 1, 3, 2):
                one(dy, dz)
            return carry

        lax.fori_loop(0, RING - 1, go, 0)
        for dy in (1, 3, 2):
            one(dy, 0)

    def send_rest():
        def one(dy, dz):
            t = lax.rem(me // RING + dy, GROUPS // RING) * RING + lax.rem(me + dz, RING)
            send_slots(CHUNKS - 1, CHUNKS, t, GROUPS * HALF, HALF)

        def go(i, carry):
            dz = jnp.where(i % 2 == 0, 1 + i // 2, RING - 1 - i // 2)
            for dy in (0, 1, 3, 2):
                one(dy, dz)
            return carry

        lax.fori_loop(0, RING - 1, go, 0)
        for dy in (1, 3, 2):
            one(dy, 0)

    send_groups(0)
    w_ring[0].wait_recv()
    w_ring[1].wait_recv()
    for k in (3, 4, 5, 6):
        w_ring[k].start()
    send_groups(1)
    w_ring[3].wait_recv()
    w_ring[4].wait_recv()
    w_ring[7].start()
    send_groups(2)
    send_groups(3)
    send_rest()
    for k in (2, 5, 6, 7):
        w_ring[k].wait_recv()
    to_tabs.wait()

    for k, ref in enumerate((wq, wk, wv)):
        for t in range(2):
            ref[t] = jnp.transpose(
                jnp.concatenate([w_all[4 * t + n, k * WIDTH:(k + 1) * WIDTH] for n in range(4)], axis=0), (1, 0))

    row2 = lax.broadcasted_iota(jnp.int32, (2 * LANES, 2 * LANES), 0)
    col2 = lax.broadcasted_iota(jnp.int32, (2 * LANES, 2 * LANES), 1)
    spread = jnp.where(row2 // WIDTH == col2 // WIDTH, 1.0 / WIDTH, 0.0).astype(BF)

    def unit_rows(rows, weights):
        wide = jnp.dot(rows, weights, preferred_element_type=F32).astype(BF).astype(F32)
        mean = jnp.dot((wide * wide).astype(BF), spread, preferred_element_type=F32)
        return (wide * lax.rsqrt(mean + EPS)).astype(BF)

    def plain_rows(rows, weights):
        return jnp.dot(rows, weights, preferred_element_type=F32).astype(BF)

    def project(s):
        def go(i, carry):
            rows = x_all[s, pl.ds(TOGETHER * i, TOGETHER)].reshape(TOGETHER * BLK, 512)
            for t in range(2):
                for ref, both in ((kp, unit_rows(rows, wk[t])), (vp, plain_rows(rows, wv[t]))):
                    for n in range(2):
                        for m in range(TOGETHER):
                            ref[s * ROWS + TOGETHER * i + m, 2 * t + n] = both[
                                m * BLK:(m + 1) * BLK, n * LANES:(n + 1) * LANES]
            return carry

        lax.fori_loop(0, ROWS // TOGETHER, go, 0)

    def project_queries():
        def go(i, carry):
            rows = x_all[mh, pl.ds(TOGETHER * i, TOGETHER)].reshape(TOGETHER * BLK, 512)
            for t in range(2):
                both = unit_rows(rows, wq[t])
                for n in range(2):
                    for m in range(TOGETHER):
                        one = both[m * BLK:(m + 1) * BLK, n * LANES:(n + 1) * LANES]
                        none = jnp.zeros_like(one)
                        q_all[TOGETHER * i + m, 2 * t + n, 0:BLK] = jnp.where(low, one, none)
                        q_all[TOGETHER * i + m, 2 * t + n, BLK:2 * BLK] = jnp.where(low, none, one)
            return carry

        lax.fori_loop(0, ROWS // TOGETHER, go, 0)

    def score(q, keys):
        return lax.dot_general(q, keys, (((1,), (1,)), ((), ())), preferred_element_type=F32)

    def blend(scores, values, p):
        weights = []
        for n in range(2):
            sharp = sharp_ref[2 * p + n]
            weights.append(jnp.exp2(
                scores[n * BLK:(n + 1) * BLK] * (sharp * (LOG2E / WIDTH)) - sharp * LOG2E).astype(BF))
        values = jnp.concatenate([values, jnp.ones_like(values)], axis=1)
        return jnp.dot(jnp.concatenate(weights, axis=0), values, preferred_element_type=F32)

    def parted(both):
        return (jnp.where(low, both[0:BLK, 0:LANES], both[BLK:2 * BLK, 0:LANES]),
                jnp.where(low, both[0:BLK, LANES:2 * LANES], both[BLK:2 * BLK, LANES:2 * LANES]))

    def near(first, last):
        def go(b, carry):
            listed = [tabs[j, mh * ROWS + b] for j in range(KL)]
            scores = [
                score(q_all[b, p], jnp.concatenate([kp[i, p] for i in listed], axis=0)) for p in range(PAIRS)]
            for p in range(PAIRS):
                both = blend(scores[p], jnp.concatenate([vp[i, p] for i in listed], axis=0), p)
                num[b, p], den[b, p] = parted(both)
            return carry

        lax.fori_loop(first, last, go, 0)

    def pass_on(k):
        c, half = (k, 0) if k < CHUNKS else (CHUNKS - 1, 1)
        halved = c == CHUNKS - 1
        count = HALF if halved else CAP
        wait_bytes(zrs[k].at[pl.ds(0, (GROUPS - 1) * count)], z_rs.at[k])

        def part(t, b, j):
            place = tabs[KL + j, t * ROWS + b]
            both = zrs[k][lax.shift_right_arithmetic(place, 1)].astype(F32)
            upper = jnp.full((8, LANES), place & 1, jnp.int32) == 0
            return jnp.where(upper, both[0:8], both[8:16])

        def go(i, carry):
            t = lax.rem(mh + jnp.where(i % 2 == 0, 4 + i // 2, 3 - i // 2), PARTS)
            if halved:
                for b in range(ROWS):
                    xs3[half, t, b] = jnp.concatenate([part(t, b, 0), part(t, b, 1)], axis=0).astype(BF)
                src, dst = xs3.at[half, t], xr3.at[half, mh]
            else:
                for e in range(ROWS * FAR):
                    xs[c, t, e] = zrs[c][tabs[KL + e % FAR, t * ROWS + e // FAR]]
                src, dst = xs.at[c, t], xr.at[mh, :, :, pl.ds(c * LANES, LANES)]

            @pl.when(i < PARTS - 1)
            def _():
                pltpu.make_async_remote_copy(
                    src_ref=src, dst_ref=dst,
                    send_sem=xr_ss.at[k], recv_sem=xr_rs.at[k] if k < CHUNKS else far_rs.at[mh],
                    device_id={"head": t}, device_id_type=MESH,
                ).start()

            return carry

        lax.fori_loop(0, PARTS, go, 0)
        if halved:
            xr3[half, mh] = xs3[half, mh]
        else:
            xr[mh, :, :, pl.ds(c * LANES, LANES)] = xs[c, mh]

    project(mh)
    x_ring[0].wait_recv()
    x_ring[1].wait_recv()
    for k in (3, 4, 5, 6):
        x_ring[k].start()
    x_ring[2].wait_recv()
    project(sib)
    project_queries()
    project(left)
    project(right)
    pass_on(0)
    x_ring[3].wait_recv()
    x_ring[4].wait_recv()
    x_ring[7].start()
    project(opp)
    x_ring[5].wait_recv()
    project(sib_left)
    x_ring[6].wait_recv()
    project(sib_right)
    pass_on(1)
    x_ring[7].wait_recv()
    project(sib_opp)
    pass_on(2)
    near(0, 4)
    pass_on(3)
    near(4, 6)
    pass_on(4)
    near(6, ROWS)
    for c in range(CHUNKS - 1):
        wait_bytes(xs.at[c, pl.ds(0, PARTS - 1)], xr_rs.at[c])
    wait_bytes(xs3.at[0, pl.ds(0, PARTS - 1)], xr_rs.at[CHUNKS - 1])

    sources = (mh, sib, left, right, sib_left, sib_right, opp, sib_opp)

    def project_far(k):
        count = ROWS * FAR * SUB
        for s in sources[k:k + 2]:
            if s is not mh:
                wait_bytes(xs3.at[1, 0], far_rs.at[s])
            first, second = xr3[0, s].astype(F32), xr3[1, s].astype(F32)
            rows = [jnp.concatenate([first[:, r:r + 8], second[:, r:r + 8]], axis=1) for r in (0, 8)]
            xr[s, :, :, pl.ds((CHUNKS - 1) * LANES, LANES)] = jnp.stack(rows, axis=1).reshape(
                ROWS * FAR, SUB, LANES).astype(BF)
        rows = jnp.concatenate([xr[s].reshape(count, 512) for s in sources[k:k + 2]], axis=0)
        for t in range(2):
            for ref, both in ((kf, unit_rows(rows, wk[t])), (vf, plain_rows(rows, wv[t]))):
                for n in range(2):
                    for m in range(2):
                        ref[2 * t + n, :, (k + m) * SUB:(k + m + 1) * SUB, :] = both[
                            m * count:(m + 1) * count, n * LANES:(n + 1) * LANES].reshape(ROWS * FAR, SUB, LANES)

    def far_keys(ref, b, p):
        return ref[p, pl.ds(FAR * b, FAR)].reshape(FAR * BLK, LANES)

    def finish(i, carry):
        units = [(FINISH * i + m, p) for m in range(FINISH) for p in range(PAIRS)]
        scores = [score(q_all[b, p], far_keys(kf, b, p)) for b, p in units]
        for (b, p), one in zip(units, scores):
            top, bottom = parted(blend(one, far_keys(vf, b, p), p))
            out_ref[pl.ds(pl.multiple_of(b * BLK, BLK), BLK), p * LANES:(p + 1) * LANES] = (
                (num[b, p] + top) / (den[b, p] + bottom)).astype(BF)
        return carry

    for k in range(0, PARTS, 2):
        project_far(k)
    lax.fori_loop(0, ROWS // FINISH, finish, 0)

    wait_bytes(rq.at[pl.ds(0, GROUPS - 1)], rq_ss)
    for c in range(CHUNKS):
        wait_bytes(xas[c].at[pl.ds(0, GROUP_BLOCKS - ROWS)], xa_ss.at[c])
        if c < CHUNKS - 1:
            wait_bytes(zs.at[c, pl.ds(0, (GROUPS - 1) * CAP)], z_ss.at[c])
            wait_bytes(xs.at[c, pl.ds(0, PARTS - 1)], xr_ss.at[c])
    for k in (CHUNKS - 1, CHUNKS):
        wait_bytes(zs.at[0, pl.ds(0, (GROUPS - 1) * HALF)], z_ss.at[k])
        wait_bytes(xs3.at[0, pl.ds(0, PARTS - 1)], xr_ss.at[k])
    for k in range(8):
        w_ring[k].wait_send()
        x_ring[k].wait_send()


def on_device(x, gain, sharp, w3, wf, targets):
    w_own = jnp.transpose(w3, (1, 2, 0)).reshape(3 * WIDTH, 512)
    vmem = pl.BlockSpec(memory_space=pltpu.VMEM)
    smem = pl.BlockSpec(memory_space=pltpu.SMEM)
    hbm = pl.BlockSpec(memory_space=pl.ANY)
    dma = pltpu.SemaphoreType.DMA
    sub = pltpu.VMEM((GROUP_BLOCKS, SUB, LANES), BF)
    landed = pltpu.VMEM((GROUPS * CAP, SUB, LANES), BF)
    half_landed = pltpu.VMEM((GROUPS * HALF, SUB, LANES), BF)
    blocks = pltpu.VMEM((GROUP_BLOCKS, PAIRS, BLK, LANES), BF)
    far_blocks = pltpu.VMEM((PAIRS, ROWS * FAR, BLK, LANES), BF)
    sums = pltpu.VMEM((ROWS, PAIRS, BLK, LANES), F32)
    weights = pltpu.VMEM((2, 512, 2 * LANES), BF)
    attended = pl.pallas_call(
        kernel,
        out_shape=pltpu.VMEM(x.shape, BF),
        in_specs=[hbm, vmem, hbm, vmem, smem],
        out_specs=vmem,
        scratch_shapes=[
            pltpu.VMEM((PARTS, ROWS, BLK, 512), BF),
            pltpu.VMEM((PARTS, 3 * WIDTH, 512), BF),
            weights, weights, weights,
            blocks, blocks, far_blocks, far_blocks,
            pltpu.VMEM((ROWS, PAIRS, 2 * BLK, LANES), BF),
            sums, sums,
            sub, sub, sub, sub, landed, landed, landed, half_landed, half_landed,
            pltpu.VMEM(x.shape, BF),
            pltpu.VMEM((CHUNKS, GROUPS * CAP, SUB, LANES), BF),
            pltpu.VMEM((CHUNKS - 1, PARTS, ROWS * FAR, SUB, LANES), BF),
            pltpu.VMEM((2, PARTS, ROWS, SUB, LANES), BF),
            pltpu.VMEM((PARTS, ROWS * FAR, SUB, 512), BF),
            pltpu.VMEM((2, PARTS, ROWS, SUB, LANES), BF),
            pltpu.VMEM((2 * 8, LANES), jnp.int32),
            pltpu.VMEM((GROUPS, 1, LANES), jnp.int32),
            pltpu.VMEM((GROUPS, 1, LANES), jnp.int32),
            pltpu.SMEM((GROUPS, 1, LANES), jnp.int32),
            pltpu.VMEM((2 * 8, LANES), jnp.int32),
            pltpu.SMEM((2 * 8, LANES), jnp.int32),
            dma((CHUNKS,)), dma((CHUNKS,)), dma(()), dma(()), dma(()), dma(()),
            dma((8,)), dma((8,)), dma((8,)), dma((8,)),
            dma((CHUNKS + 1,)), dma((CHUNKS + 1,)), dma((CHUNKS + 1,)), dma((CHUNKS,)), dma((PARTS,)),
            dma((2,)),
        ],
        compiler_params=pltpu.CompilerParams(
            collective_id=0, has_side_effects=True, vmem_limit_bytes=57 * 2**20),
        name="block_sparse_layer",
    )(x, gain.reshape(1, 512), w_own, jnp.transpose(targets), sharp)
    return jnp.dot(attended, wf, preferred_element_type=F32).astype(BF)


def solution(mesh):
    placed = (P(("seq", "head"), None), P(), P(), P(None, None, "head"), P(), P("seq", None))
    return jax.shard_map(
        on_device, mesh=mesh, in_specs=placed, out_specs=P(("seq", "head"), None), check_vma=False
    )
```

profile of v0, /device:TPU:6, one launch (start us, length us, event | category | flops | bytes accessed | tf_op | source)
XLA Modules:
  0.0 104.2 jit_solution(16751977639402120685)
XLA Ops:
  0.0 0.0 copy-start
  0.0 102.5 %block_sparse_layer.1 = bf16[1024,512]{1,0:T(8,128)(2,1)S(1)} custom-call(bf16[1024,512]{1,0:T(8,128)(2,1)} %x_ref.1, f32[1,512]{1,0:T(1,128)} %bitcast.9, bf16[192,512]{1,0:T(8,128)(2,1)} %bitcast.7, s32[12,64]{1,0:T(8,128)} %bitcast.8, f32[8]{0:T(128)} %sharp_ref.1), custom_call_target="tpu_custom_call" | custom-call | tf_op jit(solution)/shard_map/block_sparse_layer/pallas_call | solution.py:476
  102.5 0.0 copy-done
  102.5 1.7 %convolution_convert_fusion = bf16[1024,512]{1,0:T(8,128)(2,1)} fusion(bf16[1024,512]{1,0:T(8,128)(2,1)S(1)} %block_sparse_layer.1, bf16[512,512]{1,0:T(8,128)(2,1)S(1)} %copy-done), kind=kOutput, calls=%fused_computation | convolution fusion | flops 537395200 | bytes 2621440 | tf_op jit(solution)/shard_map/dot_general | solution.py:510
Async XLA Ops:
  0.0 102.5 %copy-start = (bf16[512,512]{1,0:T(8,128)(2,1)S(1)}, bf16[512,512]{1,0:T(8,128)(2,1)}, u32[]{:S(2)}) copy-start(bf16[512,512]{1,0:T(8,128)(2,1)} %param.10) | copy-start | bytes 1572868
where the time goes:
time: 104 us
  Pallas kernels  102 us (98%)
  matrix products  1.68 us (2%)
    pallas_call x1, Pallas kernels, on_device(): pl.pallas_call(kernel, out_shape=pltpu.VMEM(x.shape, BF), in_specs=[hbm,...  102 us

commit v1 on v0

--- a/solution.py
+++ b/solution.py
@@ -242,7 +242,7 @@
             send_slots(CHUNKS - 1, CHUNKS, t, GROUPS * HALF, HALF)
 
         def go(i, carry):
-            dz = jnp.where(i % 2 == 0, 1 + i // 2, RING - 1 - i // 2)
+            dz = jnp.where(i % 2 == 0, RING // 2 + i // 2, RING // 2 - 1 - i // 2)
             for dy in (0, 1, 3, 2):
                 one(dy, dz)
             return carry

time: 104 us -> 104 us (level)
  no operation moved by 1% of the time
where the time goes in v1:
time: 104 us
  Pallas kernels  102 us (98%)
  matrix products  1.68 us (2%)
    pallas_call x1, Pallas kernels, on_device(): pl.pallas_call(kernel, out_shape=pltpu.VMEM(x.shape, BF), in_specs=[hbm,...  102 us

profile of v1, /device:TPU:6, one launch (start us, length us, event | category | flops | bytes accessed | tf_op | source)
XLA Modules:
  0.0 104.2 jit_solution(8333608384939791723)
XLA Ops:
  0.0 0.0 copy-start
  0.0 102.5 %block_sparse_layer.1 = bf16[1024,512]{1,0:T(8,128)(2,1)S(1)} custom-call(bf16[1024,512]{1,0:T(8,128)(2,1)} %x_ref.1, f32[1,512]{1,0:T(1,128)} %bitcast.9, bf16[192,512]{1,0:T(8,128)(2,1)} %bitcast.7, s32[12,64]{1,0:T(8,128)} %bitcast.8, f32[8]{0:T(128)} %sharp_ref.1), custom_call_target="tpu_custom_call" | custom-call | tf_op jit(solution)/shard_map/block_sparse_layer/pallas_call | solution.py:476
  102.5 0.0 copy-done
  102.5 1.7 %convolution_convert_fusion = bf16[1024,512]{1,0:T(8,128)(2,1)} fusion(bf16[1024,512]{1,0:T(8,128)(2,1)S(1)} %block_sparse_layer.1, bf16[512,512]{1,0:T(8,128)(2,1)S(1)} %copy-done), kind=kOutput, calls=%fused_computation | convolution fusion | flops 537395200 | bytes 2621440 | tf_op jit(solution)/shard_map/dot_general | solution.py:510
Async XLA Ops:
  0.0 102.5 %copy-start = (bf16[512,512]{1,0:T(8,128)(2,1)S(1)}, bf16[512,512]{1,0:T(8,128)(2,1)}, u32[]{:S(2)}) copy-start(bf16[512,512]{1,0:T(8,128)(2,1)} %param.10) | copy-start | bytes 1572868
